TPU v7x, 512 devices: a whole 4x8x8 slice. The times are simulated.
512 devices in a mesh: tm: 512 (over x, y, z, core).
Axes of the slice: x: 4, y: 8, z: 8, core: 2. Of those that a mesh axis runs over, the one named last changes fastest.
Arguments:
- features: bfloat16 [65536, 768], P('tm'), may hold values from -256 to 256
- qkv_flat: bfloat16 [13824, 128], P('tm'), may hold values from -0.21875 to 0.21875
- out_flat: bfloat16 [4608, 128], P('tm'), may hold values from -0.21875 to 0.21875
- level_slope: float32 [12], replicated, may hold values from 0.85 to 1.4
Outputs:
- mixed: bfloat16 [65536, 768], P('tm')
All inputs are finite; a program needn't handle non-finite values.
Results may differ from a plain program's by a relative error of at most 0.012.
Values may be sent and summed in bfloat16 or wider, within the bound.
A program may use at most 64 MiB of HBM per device.

v0:
```python
import math

import jax
import jax.numpy as jnp
from jax import lax
from jax.sharding import PartitionSpec as P

D = 768
HEADS = 12
HEAD_DIM = 64
BLOCK = 16


score_scale = 0.125
log_two = math.log(2.0)


def from_partner(block, axis, stride):
    count = lax.axis_size(axis)
    route = []
    for low in range(count):
        high = low | 1 << stride
        if high != low and high < count:
            route += [(low, high), (high, low)]
    return lax.ppermute(block, axis, route)


def pair_mean(block):
    halves = block.reshape(block.shape[0] // 2, 2, block.shape[1])
    return (halves[:, 0] + halves[:, 1]) * 0.5


def pair_stats(queries, key_rows, val_rows, at_level, slope):
    row_count = queries.shape[0]
    groups = row_count // (2 * BLOCK)
    block_shape = (groups, 2, BLOCK, HEADS, HEAD_DIM)
    q_blocks = queries.reshape(block_shape)
    k_blocks = key_rows.reshape(block_shape)
    v_blocks = val_rows.reshape(block_shape)
    if at_level == 0:
        key_pair = k_blocks.reshape(groups, 2 * BLOCK, HEADS, HEAD_DIM)
        val_pair = v_blocks.reshape(groups, 2 * BLOCK, HEADS, HEAD_DIM)
        scores = (
            jnp.einsum("gpihd,gjhd->gpihj", q_blocks, key_pair, preferred_element_type=jnp.float32)
            * score_scale
        )
        maxima = jnp.max(scores, axis=-1)
        powers = jnp.exp(scores - maxima[..., None])
        numerator = jnp.einsum(
            "gpihj,gjhd->gpihd",
            powers.astype(jnp.bfloat16),
            val_pair,
            preferred_element_type=jnp.float32,
        )
    else:
        level_bias = at_level * log_two * (1.0 - slope)
        scores = (
            jnp.einsum(
                "gpihd,gpjhd->gpihj", q_blocks, k_blocks[:, ::-1], precision=lax.Precision.HIGHEST
            )
            * score_scale
            + level_bias[:, None]
        )
        maxima = jnp.max(scores, axis=-1)
        powers = jnp.exp(scores - maxima[..., None])
        numerator = jnp.einsum(
            "gpihj,gpjhd->gpihd", powers, v_blocks[:, ::-1], precision=lax.Precision.HIGHEST
        )
    denominator = jnp.sum(powers, axis=-1)
    return (
        maxima.reshape(row_count, HEADS),
        numerator.reshape(row_count, HEADS, HEAD_DIM),
        denominator.reshape(row_count, HEADS),
    )


def cross_stats(queries, key_rows, val_rows, at_level, slope):
    row_count = queries.shape[0]
    q_heads = queries.reshape(row_count, HEADS, HEAD_DIM)
    k_heads = key_rows.reshape(BLOCK, HEADS, HEAD_DIM)
    v_heads = val_rows.reshape(BLOCK, HEADS, HEAD_DIM)
    level_bias = at_level * log_two * (1.0 - slope)
    scores = (
        jnp.einsum("ihd,jhd->ihj", q_heads, k_heads, precision=lax.Precision.HIGHEST) * score_scale
        + level_bias[:, None]
    )
    maxima = jnp.max(scores, axis=-1)
    powers = jnp.exp(scores - maxima[..., None])
    numerator = jnp.einsum("ihj,jhd->ihd", powers, v_heads, precision=lax.Precision.HIGHEST)
    return (maxima, numerator, jnp.sum(powers, axis=-1))


def combine(state, stats, factor):
    old_top, old_num, old_den = state
    new_top, new_num, new_den = [jnp.repeat(member, factor, axis=0) for member in stats]
    highest = jnp.maximum(old_top, new_top)
    old_scale = jnp.exp(old_top - highest)
    new_scale = jnp.exp(new_top - highest)
    return (
        highest,
        old_num * old_scale[..., None] + new_num * new_scale[..., None],
        old_den * old_scale + new_den * new_scale,
    )


def local_levels(projected, slope):
    row_count = projected.shape[0]
    queries = projected[:, :D]
    key_rows = projected[:, D : 2 * D]
    val_rows = projected[:, 2 * D :]
    state = pair_stats(queries, key_rows, val_rows, 0, slope)
    coarse = (
        queries.astype(jnp.float32),
        key_rows.astype(jnp.float32),
        val_rows.astype(jnp.float32),
    )
    at_level = 1
    while BLOCK << at_level <= row_count:
        coarse = tuple((pair_mean(member) for member in coarse))
        if BLOCK << at_level + 1 <= row_count:
            state = combine(
                state, pair_stats(coarse[0], coarse[1], coarse[2], at_level, slope), 1 << at_level
            )
        at_level += 1
    return (state, coarse)


def shards(features, qkv_flat, out_flat, level_slope):
    tok_rows = features.shape[0]
    devices = lax.axis_size("tm")
    my_index = lax.axis_index("tm")
    bit_count = devices.bit_length() - 1
    base_level = (tok_rows // BLOCK).bit_length() - 1
    qkv_all, out_all = (
        lax.all_gather(qkv_flat, "tm", axis=0, tiled=True),
        lax.all_gather(out_flat, "tm", axis=0, tiled=True),
    )
    projected = jnp.dot(
        features, qkv_all.reshape(D, 3 * D), preferred_element_type=jnp.float32
    ).astype(jnp.bfloat16)
    state, group = local_levels(projected, level_slope)
    for bit_no in range(bit_count):
        other = from_partner(group, "tm", bit_no)
        row_span = max(BLOCK >> bit_no, 1)
        row_start = my_index % (1 << bit_no) * BLOCK // (1 << bit_no)
        queries = lax.dynamic_slice_in_dim(group[0], row_start, row_span, 0)
        state = combine(
            state,
            cross_stats(queries, other[1], other[2], base_level + bit_no, level_slope),
            tok_rows // row_span,
        )
        if bit_no + 1 < bit_count:
            is_lower = my_index // (1 << bit_no) % 2 == 0
            group = tuple(
                (
                    pair_mean(
                        jnp.where(
                            is_lower,
                            jnp.concatenate([own_part, peer_part]),
                            jnp.concatenate([peer_part, own_part]),
                        )
                    )
                    for own_part, peer_part in zip(group, other)
                )
            )
    highest, numerator, denominator = state
    attended = (numerator / denominator[..., None]).reshape(tok_rows, D).astype(jnp.bfloat16)
    return jnp.dot(attended, out_all.reshape(D, D), preferred_element_type=jnp.float32).astype(
        jnp.bfloat16
    )


def solution(mesh):
    in_specs = (P("tm", None), P("tm", None), P("tm", None), P())
    out_specs = P("tm", None)
    return jax.shard_map(shards, mesh=mesh, in_specs=in_specs, out_specs=out_specs, check_vma=False)
```

profile of v0, /device:TPU:1, one launch (start us, length us, event | category | flops | bytes accessed | tf_op | source)
XLA Modules:
  0.0 437.9 jit_solution(194071309638208867)
XLA Ops:
  9.7 123.0 %all-gather.7.cloned.1.call-done = bf16[512,9,128]{2,1,0:T(8,128)(2,1)} async-done(((bf16[1,9,128]{2,1,0:T(8,128)(2,1)}), bf16[512,9,128]{2,1,0:T(8,128)(2,1)}) %all-gather.7.cloned.1.call-update) | async-done | bytes 1179664 | tf_op jit(solution)/shard_map/all_gather | solution.py:136
  132.7 3.0 reshape.2074
  135.7 116.2 %all-gather.5.cloned.1.call-done = bf16[512,27,128]{2,1,0:T(8,128)(2,1)} async-done(((bf16[1,27,128]{2,1,0:T(8,128)(2,1)}), bf16[512,27,128]{2,1,0:T(8,128)(2,1)}) %all-gather.5.cloned.1.call-update) | async-done | bytes 3538960 | tf_op jit(solution)/shard_map/all_gather | solution.py:135
  251.9 7.7 %reshape.1995 = bf16[768,2304]{1,0:T(8,128)(2,1)} reshape(bf16[512,27,128]{2,1,0:T(8,128)(2,1)} %all-gather.5.cloned.1.call-done) | data formatting | bytes 7077888 | tf_op jit(solution)/shard_map/reshape | solution.py:139
  259.6 2.6 convolution_convert_fusion
  308.5 2.8 collective-permute-start.2
  317.6 3.6 collective-permute-start.9
  321.4 2.6 collective-permute-start.5
  327.5 3.6 collective-permute-start.7
  333.1 4.9 %collective-permute-start.8 = (f32[16,768]{1,0:T(8,128)S(1)}, f32[16,768]{1,0:T(8,128)S(1)}, u32[]{:S(2)}, u32[]{:S(2)}) collective-permute-start(f32[16,768]{1,0:T(8,128)S(1)} %fusion.118), channel_id=1, source_target_pairs={{0,8},{8,0},{1,9},{9,1},{2,10},{10,2},{3,11},{11,3},{4,12},{12,4},... | collective-permute-start | bytes 147464 | tf_op jit(solution)/shard_map/ppermute | solution.py:25
  338.0 4.2 collective-permute-start.12
  345.0 4.9 %collective-permute-start.10 = (f32[16,768]{1,0:T(8,128)S(1)}, f32[16,768]{1,0:T(8,128)S(1)}, u32[]{:S(2)}, u32[]{:S(2)}) collective-permute-start(f32[16,768]{1,0:T(8,128)S(1)} %fusion.115), channel_id=1, source_target_pairs={{0,8},{8,0},{1,9},{9,1},{2,10},{10,2},{3,11},{11,3},{4,12},{12,4},... | collective-permute-start | bytes 147464 | tf_op jit(solution)/shard_map/ppermute | solution.py:25
  353.4 3.1 collective-permute-start.11
  364.3 3.7 collective-permute-start.18
  374.4 3.7 collective-permute-start.16
  378.7 4.6 %collective-permute-start.21 = (f32[16,768]{1,0:T(8,128)S(1)}, f32[16,768]{1,0:T(8,128)}, u32[]{:S(2)}, u32[]{:S(2)}) collective-permute-start(f32[16,768]{1,0:T(8,128)S(1)} %bitcast.351), channel_id=1, source_target_pairs={{0,64},{64,0},{1,65},{65,1},{2,66},{66,2},{3,67},{67,3},{4,68},{68... | collective-permute-start | bytes 147464 | tf_op jit(solution)/shard_map/ppermute | solution.py:25
  383.4 4.6 %collective-permute-start.17 = (f32[16,768]{1,0:T(8,128)S(1)}, f32[16,768]{1,0:T(8,128)S(1)}, u32[]{:S(2)}, u32[]{:S(2)}) collective-permute-start(f32[16,768]{1,0:T(8,128)S(1)} %fusion.103), channel_id=1, source_target_pairs={{0,64},{64,0},{1,65},{65,1},{2,66},{66,2},{3,67},{67,3},{4,68},{68... | collective-permute-start | bytes 147464 | tf_op jit(solution)/shard_map/ppermute | solution.py:25
  389.6 4.6 %collective-permute-start.19 = (f32[16,768]{1,0:T(8,128)S(1)}, f32[16,768]{1,0:T(8,128)S(1)}, u32[]{:S(2)}, u32[]{:S(2)}) collective-permute-start(f32[16,768]{1,0:T(8,128)S(1)} %fusion.100), channel_id=1, source_target_pairs={{0,64},{64,0},{1,65},{65,1},{2,66},{66,2},{3,67},{67,3},{4,68},{68... | collective-permute-start | bytes 147464 | tf_op jit(solution)/shard_map/ppermute | solution.py:25
  395.6 2.5 collective-permute-start.24
  398.3 2.8 collective-permute-start.20
  403.3 2.7 collective-permute-start.22
  408.2 4.3 collective-permute-start.23
  416.3 2.5 collective-permute-start.25
  424.4 5.4 %fusion.36 = bf16[128,12,64]{2,0,1:T(8,128)(2,1)S(1)} fusion(f32[128,12,64]{2,0,1:T(8,128)S(1)} %bitcast.331, f32[128,12,64]{2,0,1:T(8,128)S(1)} %bitcast.330, f32[4,2,16,12,64]{4,2,1,0,3:T(8,128)S(1)} %copy.515, f32[128,12]{0,1:T(8,128)S(1)} %get-tuple-element.9, f32[128,12]{0,1:T(8,128)S(1)} %get-tuple-element.31, f32[12,64]{1,0:T(8,128)S(1)} %bitcast.365, ...), kind=kLoop, calls=%fused_computation.57 | loop fusion | flops 3440640 | bytes 1625088 | tf_op jit(solution)/shard_map/convert_element_type | solution.py:167
  (334 shorter events, 98.5 us)
Async XLA Ops:
  6.5 126.2 %all-gather.7.cloned.1.call-start = ((), (), s32[]{:S(2)}) async-start(), calls=%async_computation.1 | async-start | bytes 2101248 | tf_op jit(solution)/shard_map/all_gather | solution.py:136
  7.3 244.6 %all-gather.5.cloned.1.call-start = ((), (), s32[]{:S(2)}) async-start(), calls=%async_computation | async-start | bytes 4202496 | tf_op jit(solution)/shard_map/all_gather | solution.py:135
  281.3 23.5 %collective-permute-start.3 = (f32[16,768]{1,0:T(8,128)}, f32[16,768]{1,0:T(8,128)}, u32[]{:S(2)}, u32[]{:S(2)}) collective-permute-start(f32[16,768]{1,0:T(8,128)} %bitcast.32), channel_id=1, source_target_pairs={{0,1},{1,0},{2,3},{3,2},{4,5},{5,4},{6,7},{7,6},{8,9},{9,8},{10,11... | collective-permute-start | bytes 147464 | tf_op jit(solution)/shard_map/ppermute | solution.py:25
  294.0 14.3 %collective-permute-start = (f32[16,768]{1,0:T(8,128)S(1)}, f32[16,768]{1,0:T(8,128)S(1)}, u32[]{:S(2)}, u32[]{:S(2)}) collective-permute-start(f32[16,768]{1,0:T(8,128)S(1)} %bitcast.355), channel_id=1, source_target_pairs={{0,1},{1,0},{2,3},{3,2},{4,5},{5,4},{6,7},{7,6},{8,9},{9,8},{10,11... | collective-permute-start | bytes 147464 | tf_op jit(solution)/shard_map/ppermute | solution.py:25
  305.8 11.7 %collective-permute-start.6 = (f32[16,768]{1,0:T(8,128)S(1)}, f32[16,768]{1,0:T(8,128)S(1)}, u32[]{:S(2)}, u32[]{:S(2)}) collective-permute-start(f32[16,768]{1,0:T(8,128)S(1)} %bitcast.337), channel_id=1, source_target_pairs={{0,2},{2,0},{1,3},{3,1},{4,6},{6,4},{5,7},{7,5},{8,10},{10,8},{9,1... | collective-permute-start | bytes 147464 | tf_op jit(solution)/shard_map/ppermute | solution.py:25
  308.5 12.8 %collective-permute-start.2 = (f32[16,768]{1,0:T(8,128)S(1)}, f32[16,768]{1,0:T(8,128)S(1)}, u32[]{:S(2)}, u32[]{:S(2)}) collective-permute-start(f32[16,768]{1,0:T(8,128)S(1)} %fusion.128), channel_id=1, source_target_pairs={{0,2},{2,0},{1,3},{3,1},{4,6},{6,4},{5,7},{7,5},{8,10},{10,8},{9,1... | collective-permute-start | bytes 147464 | tf_op jit(solution)/shard_map/ppermute | solution.py:25
  317.6 13.5 %collective-permute-start.9 = (f32[16,768]{1,0:T(8,128)S(1)}, f32[16,768]{1,0:T(8,128)}, u32[]{:S(2)}, u32[]{:S(2)}) collective-permute-start(f32[16,768]{1,0:T(8,128)S(1)} %bitcast.343), channel_id=1, source_target_pairs={{0,4},{4,0},{1,5},{5,1},{2,6},{6,2},{3,7},{7,3},{8,12},{12,8},{9,1... | collective-permute-start | bytes 147464 | tf_op jit(solution)/shard_map/ppermute | solution.py:25
  321.4 10.7 %collective-permute-start.5 = (f32[16,768]{1,0:T(8,128)S(1)}, f32[16,768]{1,0:T(8,128)S(1)}, u32[]{:S(2)}, u32[]{:S(2)}) collective-permute-start(f32[16,768]{1,0:T(8,128)S(1)} %fusion.123), channel_id=1, source_target_pairs={{0,4},{4,0},{1,5},{5,1},{2,6},{6,2},{3,7},{7,3},{8,12},{12,8},{9,1... | collective-permute-start | bytes 147464 | tf_op jit(solution)/shard_map/ppermute | solution.py:25
  327.5 14.7 %collective-permute-start.7 = (f32[16,768]{1,0:T(8,128)S(1)}, f32[16,768]{1,0:T(8,128)S(1)}, u32[]{:S(2)}, u32[]{:S(2)}) collective-permute-start(f32[16,768]{1,0:T(8,128)S(1)} %fusion.120), channel_id=1, source_target_pairs={{0,4},{4,0},{1,5},{5,1},{2,6},{6,2},{3,7},{7,3},{8,12},{12,8},{9,1... | collective-permute-start | bytes 147464 | tf_op jit(solution)/shard_map/ppermute | solution.py:25
  333.1 20.2 %collective-permute-start.8 = (f32[16,768]{1,0:T(8,128)S(1)}, f32[16,768]{1,0:T(8,128)S(1)}, u32[]{:S(2)}, u32[]{:S(2)}) collective-permute-start(f32[16,768]{1,0:T(8,128)S(1)} %fusion.118), channel_id=1, source_target_pairs={{0,8},{8,0},{1,9},{9,1},{2,10},{10,2},{3,11},{11,3},{4,12},{12,4},... | collective-permute-start | bytes 147464 | tf_op jit(solution)/shard_map/ppermute | solution.py:25
  338.0 12.0 %collective-permute-start.12 = (f32[16,768]{1,0:T(8,128)S(1)}, f32[16,768]{1,0:T(8,128)}, u32[]{:S(2)}, u32[]{:S(2)}) collective-permute-start(f32[16,768]{1,0:T(8,128)S(1)} %bitcast.345), channel_id=1, source_target_pairs={{0,8},{8,0},{1,9},{9,1},{2,10},{10,2},{3,11},{11,3},{4,12},{12,4},... | collective-permute-start | bytes 147464 | tf_op jit(solution)/shard_map/ppermute | solution.py:25
  345.0 13.5 %collective-permute-start.10 = (f32[16,768]{1,0:T(8,128)S(1)}, f32[16,768]{1,0:T(8,128)S(1)}, u32[]{:S(2)}, u32[]{:S(2)}) collective-permute-start(f32[16,768]{1,0:T(8,128)S(1)} %fusion.115), channel_id=1, source_target_pairs={{0,8},{8,0},{1,9},{9,1},{2,10},{10,2},{3,11},{11,3},{4,12},{12,4},... | collective-permute-start | bytes 147464 | tf_op jit(solution)/shard_map/ppermute | solution.py:25
  351.1 13.0 %collective-permute-start.15 = (f32[16,768]{1,0:T(8,128)S(1)}, f32[16,768]{1,0:T(8,128)S(1)}, u32[]{:S(2)}, u32[]{:S(2)}) collective-permute-start(f32[16,768]{1,0:T(8,128)S(1)} %bitcast.347), channel_id=1, source_target_pairs={{0,16},{16,0},{1,17},{17,1},{2,18},{18,2},{3,19},{19,3},{4,20},{20... | collective-permute-start | bytes 147464 | tf_op jit(solution)/shard_map/ppermute | solution.py:25
  353.4 14.6 %collective-permute-start.11 = (f32[16,768]{1,0:T(8,128)S(1)}, f32[16,768]{1,0:T(8,128)S(1)}, u32[]{:S(2)}, u32[]{:S(2)}) collective-permute-start(f32[16,768]{1,0:T(8,128)S(1)} %fusion.113), channel_id=1, source_target_pairs={{0,16},{16,0},{1,17},{17,1},{2,18},{18,2},{3,19},{19,3},{4,20},{20... | collective-permute-start | bytes 147464 | tf_op jit(solution)/shard_map/ppermute | solution.py:25
  358.7 15.5 %collective-permute-start.13 = (f32[16,768]{1,0:T(8,128)S(1)}, f32[16,768]{1,0:T(8,128)S(1)}, u32[]{:S(2)}, u32[]{:S(2)}) collective-permute-start(f32[16,768]{1,0:T(8,128)S(1)} %fusion.110), channel_id=1, source_target_pairs={{0,16},{16,0},{1,17},{17,1},{2,18},{18,2},{3,19},{19,3},{4,20},{20... | collective-permute-start | bytes 147464 | tf_op jit(solution)/shard_map/ppermute | solution.py:25
  364.3 14.2 %collective-permute-start.18 = (f32[16,768]{1,0:T(8,128)S(1)}, f32[16,768]{1,0:T(8,128)S(1)}, u32[]{:S(2)}, u32[]{:S(2)}) collective-permute-start(f32[16,768]{1,0:T(8,128)S(1)} %bitcast.349), channel_id=1, source_target_pairs={{0,32},{32,0},{1,33},{33,1},{2,34},{34,2},{3,35},{35,3},{4,36},{36... | collective-permute-start | bytes 147464 | tf_op jit(solution)/shard_map/ppermute | solution.py:25
  368.2 15.0 %collective-permute-start.14 = (f32[16,768]{1,0:T(8,128)S(1)}, f32[16,768]{1,0:T(8,128)S(1)}, u32[]{:S(2)}, u32[]{:S(2)}) collective-permute-start(f32[16,768]{1,0:T(8,128)S(1)} %fusion.108), channel_id=1, source_target_pairs={{0,32},{32,0},{1,33},{33,1},{2,34},{34,2},{3,35},{35,3},{4,36},{36... | collective-permute-start | bytes 147464 | tf_op jit(solution)/shard_map/ppermute | solution.py:25
  374.4 15.1 %collective-permute-start.16 = (f32[16,768]{1,0:T(8,128)S(1)}, f32[16,768]{1,0:T(8,128)S(1)}, u32[]{:S(2)}, u32[]{:S(2)}) collective-permute-start(f32[16,768]{1,0:T(8,128)S(1)} %fusion.105), channel_id=1, source_target_pairs={{0,32},{32,0},{1,33},{33,1},{2,34},{34,2},{3,35},{35,3},{4,36},{36... | collective-permute-start | bytes 147464 | tf_op jit(solution)/shard_map/ppermute | solution.py:25
  378.7 15.9 %collective-permute-start.21 = (f32[16,768]{1,0:T(8,128)S(1)}, f32[16,768]{1,0:T(8,128)}, u32[]{:S(2)}, u32[]{:S(2)}) collective-permute-start(f32[16,768]{1,0:T(8,128)S(1)} %bitcast.351), channel_id=1, source_target_pairs={{0,64},{64,0},{1,65},{65,1},{2,66},{66,2},{3,67},{67,3},{4,68},{68... | collective-permute-start | bytes 147464 | tf_op jit(solution)/shard_map/ppermute | solution.py:25
  383.4 14.7 %collective-permute-start.17 = (f32[16,768]{1,0:T(8,128)S(1)}, f32[16,768]{1,0:T(8,128)S(1)}, u32[]{:S(2)}, u32[]{:S(2)}) collective-permute-start(f32[16,768]{1,0:T(8,128)S(1)} %fusion.103), channel_id=1, source_target_pairs={{0,64},{64,0},{1,65},{65,1},{2,66},{66,2},{3,67},{67,3},{4,68},{68... | collective-permute-start | bytes 147464 | tf_op jit(solution)/shard_map/ppermute | solution.py:25
  389.6 13.4 %collective-permute-start.19 = (f32[16,768]{1,0:T(8,128)S(1)}, f32[16,768]{1,0:T(8,128)S(1)}, u32[]{:S(2)}, u32[]{:S(2)}) collective-permute-start(f32[16,768]{1,0:T(8,128)S(1)} %fusion.100), channel_id=1, source_target_pairs={{0,64},{64,0},{1,65},{65,1},{2,66},{66,2},{3,67},{67,3},{4,68},{68... | collective-permute-start | bytes 147464 | tf_op jit(solution)/shard_map/ppermute | solution.py:25
  395.6 10.7 %collective-permute-start.24 = (f32[16,768]{1,0:T(8,128)S(1)}, f32[16,768]{1,0:T(8,128)}, u32[]{:S(2)}, u32[]{:S(2)}) collective-permute-start(f32[16,768]{1,0:T(8,128)S(1)} %bitcast.353), channel_id=1, source_target_pairs={{0,128},{128,0},{1,129},{129,1},{2,130},{130,2},{3,131},{131,3},{4... | collective-permute-start | bytes 147464 | tf_op jit(solution)/shard_map/ppermute | solution.py:25
  403.3 12.8 %collective-permute-start.22 = (f32[16,768]{1,0:T(8,128)S(1)}, f32[16,768]{1,0:T(8,128)S(1)}, u32[]{:S(2)}, u32[]{:S(2)}) collective-permute-start(f32[16,768]{1,0:T(8,128)S(1)} %fusion.95), channel_id=1, source_target_pairs={{0,128},{128,0},{1,129},{129,1},{2,130},{130,2},{3,131},{131,3},{4... | collective-permute-start | bytes 147464 | tf_op jit(solution)/shard_map/ppermute | solution.py:25
  408.2 10.9 %collective-permute-start.23 = (f32[16,768]{1,0:T(8,128)S(1)}, f32[16,768]{1,0:T(8,128)S(1)}, u32[]{:S(2)}, u32[]{:S(2)}) collective-permute-start(f32[16,768]{1,0:T(8,128)S(1)} %fusion.93), channel_id=1, source_target_pairs={{0,256},{256,0},{1,257},{257,1},{2,258},{258,2},{3,259},{259,3},{4... | collective-permute-start | bytes 147464 | tf_op jit(solution)/shard_map/ppermute | solution.py:25
  (22 other events, 465.3 us)
Sparse Core Ops, SparseCore 0:
  11.5 121.1 all-gather.6
  136.9 114.9 all-gather.4
where the time goes:
time: 446 us; the launch traced here: 438 us
  waiting for transfers between devices  242 us (54%)
  starting transfers between devices  84.2 us (19%)
  local copies, waits for them, and re-layouts  44.2 us (10%)
  other arithmetic  32.8 us (7%)
  matrix products  18.8 us (4%)
  between operations  15.7 us (4%)
    all_gather x1, waiting for transfers between devices, shards(): lax.all_gather(out_flat, 'tm', axis=0, tiled=True)  123 us
    all_gather x1, waiting for transfers between devices, shards(): lax.all_gather(qkv_flat, 'tm', axis=0, tiled=True)  116 us
    ppermute x26, starting transfers between devices, from_partner(): return lax.ppermute(block, axis, route)  84.2 us
  transfers between devices with their start and end apart: 28, of which 3 were waited for; matrix products, arithmetic and copies ran while one was open for 13% of the time, Pallas kernels for 0%

commit v1 on v0

v1 whole, which is shorter than its diff:
```python
import math

import jax
import jax.numpy as jnp
from jax import lax
from jax.experimental import pallas as pl
from jax.experimental.pallas import tpu as pltpu
from jax.sharding import PartitionSpec as P

D = 768
HEADS = 12
HEAD_DIM = 64
BLOCK = 16
TOK = 128
NX, NY, NZ = 4, 8, 8
NG = NY // 2
SEL = 12
SEL_A = 8
RAW = 48
KROWS = 48
LOG_TWO = math.log(2.0)
F32, BF16, I32 = jnp.float32, jnp.bfloat16, jnp.int32
MESH = pl.DeviceIdType.MESH


def iota(shape, dim):
    return lax.broadcasted_iota(I32, shape, dim)


def pick(condition, value=1.0):
    return jnp.where(condition, value, 0.0).astype(BF16)


def mm(a, b):
    return jnp.dot(a, b, preferred_element_type=F32)


def mm_nt(a, b):
    return lax.dot_general(a, b, (((1,), (1,)), ((), ())), preferred_element_type=F32)


def third(value):
    return lax.shift_right_logical(value * 171, 9)


def line_rows(place):
    row, col = iota((64, 128), 0), iota((64, 128), 1)
    r = row & 15
    first = pick((row < 16) & (col == 16 * (place ^ 1) + r))
    second = pick((row >= 16) & (row < 32) & ((col >> 1) == 16 * ((place >> 1) ^ 1) + r), 0.5)
    fourth = pick((row >= 32) & (row < 48) & ((col >> 2) == 16 * ((place >> 2) ^ 1) + r), 0.25)
    whole = pick((row >= 48) & ((col >> 3) == r), 0.125)
    return first + second + fourth + whole


def body(
    x_ref, qkv_ref, out_ref, slope_ref, o_ref,
    raw, stage, gather, buf_a, buf_b, feat3, feat4, feat7, feat10,
    rows, perm, expand, q_all, k_all, v_all, q_exp, attended,
    send, recv,
):
    me = lax.axis_index("tm")
    x, y, z, c = me // 128, (me // 16) % 8, (me // 2) % 8, me % 2
    yg, yp = y // 2, y % 2

    def at(px, py, pz, pc):
        return ((px * NY + py) * NZ + pz) * 2 + pc

    sibling = at(x, y, z, 1 - c)
    z_line = [at(x, y, (z + j) % 8, c) for j in range(1, 8)]
    z_other = [at(x, y + 1 - 2 * yp, (z + j) % 8, c) for j in range(8)]
    y_line = [at(x, (y + j) % 8, z, c) for j in range(1, 8)]
    y_even = [at(x, (y + 2 * j) % 8, z, c) for j in range(1, 4)]
    x_line = [at((x + j) % 4, y, z, c) for j in range(1, 4)]

    barrier = pltpu.get_barrier_semaphore()
    greet = [sibling] + z_line + z_other + y_line + x_line
    for other in greet:
        pl.semaphore_signal(barrier, inc=1, device_id=(other,), device_id_type=MESH)

    count = [0]

    def copy(src, dst, device):
        slot = count[0]
        count[0] += 1
        made = pltpu.make_async_remote_copy(
            src_ref=src, dst_ref=dst, send_sem=send.at[slot], recv_sem=recv.at[slot],
            device_id=(device,), device_id_type=MESH,
        )
        made.start()
        sent.append(made)
        return made

    sent = []

    stage[...] = jnp.zeros((RAW, 128), F32)
    stage[0:27, :] = qkv_ref[...].astype(F32)
    stage[32:41, :] = out_ref[...].astype(F32)
    raw[c] = stage[...].astype(BF16)
    tokens = x_ref[...]
    rows[0:128, :] = tokens
    row, col = iota((16, 128), 0), iota((16, 128), 1)
    feat3[c] = mm(pick((col >> 3) == row, 0.125), tokens).astype(BF16)
    row, col = iota((RAW, 2 * RAW), 0), iota((RAW, 2 * RAW), 1)
    k = third(row) >> 2
    rest = row - 12 * k
    s = third(rest)
    j = rest - 3 * s
    flat = jnp.where(s < 3, k * 18 + s * 6, k * 6) + 3 * c + j
    half = jnp.where(s < 3, 27, 9)
    side = (flat >= half).astype(I32)
    source = side * RAW + flat - half * side + jnp.where(s < 3, 0, 32)
    choose = pick((row < 36) & (col == source))
    row, col = iota((SEL * KROWS, 16 * RAW), 0), iota((SEL * KROWS, 16 * RAW), 1)
    n = third(row >> 4)
    rest = row - 48 * n
    i = third(rest)
    k = rest - 3 * i
    perm[...] = pick(col == i * 48 + k * 12 + n)
    for level in range(1, 12):
        row, col = iota((128, 144), 0), iota((128, 144), 1)
        if level < 8:
            hit = (col < 128) & ((col >> level) == (row >> level))
            expand[pl.ds((level - 1) * 128, 128), :] = pick(hit, 0.125 / (1 << level))
        else:
            expand[pl.ds((level - 1) * 128, 128), :] = pick(col == 128 + level - 8, 0.125)

    pl.semaphore_wait(barrier, len(greet))

    a = copy(raw.at[c], raw.at[c], sibling)
    b = copy(feat3.at[c], feat3.at[c], sibling)
    a.wait_recv()
    spot = yp * 8 + z
    gather[spot] = mm(choose, raw[...].reshape(2 * RAW, 128)).astype(BF16)
    first = [copy(gather.at[spot], gather.at[spot], other) for other in z_line + z_other]
    b.wait_recv()
    row, col = iota((16, 32), 0), iota((16, 32), 1)
    feat4[z] = mm(pick((col >> 1) == row, 0.5), feat3[...].reshape(32, D)).astype(BF16)
    line = [copy(feat4.at[z], feat4.at[z], other) for other in z_line]
    rows[144:160, :] = feat3[1 - c]

    for made in first:
        made.wait_recv()
    chunk = mm(perm[...], gather[...].reshape(16 * RAW, 128)).astype(BF16)
    buf_a[c, x, yg] = chunk[: SEL_A * KROWS]
    buf_b[c, yg, x] = chunk[SEL_A * KROWS :]
    a2 = [copy(buf_a.at[c, x, yg], buf_a.at[c, x, yg], other) for other in y_even]
    b2 = [copy(buf_b.at[c, yg, x], buf_b.at[c, yg, x], other) for other in x_line]

    for made in line:
        made.wait_recv()
    z_rows = feat4[...].reshape(128, D)
    found = mm(line_rows(z), z_rows).astype(BF16)
    rows[160:208, :] = found[:48]
    feat7[y] = found[48:]
    line = [copy(feat7.at[y], feat7.at[y], other) for other in y_line]
    row, col = iota((16, 128), 0), iota((16, 128), 1)
    span = row + 4
    means = (
        pick((row == 0) & ((col >> 4) == z), 1 / 16)
        + pick((row == 1) & ((col >> 5) == (z >> 1)), 1 / 32)
        + pick((row == 2) & ((col >> 6) == (z >> 2)), 1 / 64)
        + pick(row == 3, 1 / 128)
    )
    rows[128:144, :] = mm(means, z_rows).astype(BF16)

    for made in a2:
        made.wait_recv()
    a3 = [copy(buf_a.at[c, x], buf_a.at[c, x], other) for other in x_line]
    across = [copy(buf_a.at[c, x], buf_a.at[c, x], sibling)]
    for made in b2:
        made.wait_recv()
    b3 = [copy(buf_b.at[c, yg], buf_b.at[c, yg], other) for other in y_even]
    across.append(copy(buf_b.at[c, yg], buf_b.at[c, yg], sibling))

    for made in line:
        made.wait_recv()
    found = mm(line_rows(y), feat7[...].reshape(128, D)).astype(BF16)
    rows[208:256, :] = found[:48]
    feat10[x] = found[48:]
    line = [copy(feat10.at[x], feat10.at[x], other) for other in x_line]
    for made in line:
        made.wait_recv()
    row, col = iota((32, 64), 0), iota((32, 64), 1)
    sides = pick((row < 16) & (col == 16 * (x ^ 1) + row)) + pick(
        (row >= 16) & ((col >> 1) == 16 * ((x >> 1) ^ 1) + row - 16), 0.5
    )
    rows[256:288, :] = mm(sides, feat10[...].reshape(64, D)).astype(BF16)

    for j, made in enumerate(a3):
        made.wait_recv()
        src = buf_a.at[c, (x + 3 - j) % 4]
        across.append(copy(src, src, sibling))
    for j, made in enumerate(b3):
        made.wait_recv()
        src = buf_b.at[c, (yg + 3 - j) % 4]
        across.append(copy(src, src, sibling))
    for made in across:
        made.wait_recv()

    def weight(kind, owner, j):
        place = kind * 3 + j
        parts = []
        for px in range(NX):
            for pg in range(NG):
                if place < SEL_A:
                    parts.append(buf_a[owner, px, pg, place * KROWS : (place + 1) * KROWS, :])
                else:
                    low = place - SEL_A
                    parts.append(buf_b[owner, pg, px, low * KROWS : (low + 1) * KROWS, :])
        return jnp.concatenate(parts, axis=0)

    def weights(kind, pair):
        blocks = [weight(kind, n // 3, n % 3) for n in (2 * pair, 2 * pair + 1)]
        return jnp.concatenate(blocks, axis=1)

    row, col = iota((96, 128), 0), iota((96, 128), 1)
    pool = pick((row < 64) & ((col >> 1) == row), 0.5) + pick(
        (row >= 64) & ((col >> 2) == row - 64), 0.25
    )
    for pair in range(3):
        lanes = slice(pair * 256, (pair + 1) * 256)
        q_all[:, lanes] = mm(rows[0:144, :], weights(0, pair)).astype(BF16)
        for kind, target in ((1, k_all), (2, v_all)):
            made = mm(rows[...], weights(kind, pair)).astype(BF16)
            target[0:128, lanes] = made[0:128]
            target[128:224, lanes] = mm(pool, made[0:128]).astype(BF16)
            target[224:368, lanes] = made[144:288]
            target[368:384, lanes] = jnp.zeros((16, 256), BF16)
        q_exp[:, lanes] = mm(expand[...], q_all[:, lanes]).astype(BF16)

    eye = pick(iota((128, 128), 0) == iota((128, 128), 1))
    lane = iota((128, 128), 1)
    key = iota((128, 128), 0)
    seen0 = (key >> 5) == (lane >> 5)
    seen1 = (key[:64] >> 4) == ((lane[:64] >> 5) ^ 1)
    seen2 = (key[:32] >> 4) == ((lane[:32] >> 6) ^ 1)
    starts = [0, 128, 192] + [224 + 16 * n for n in range(9)] + [368]
    for pair in range(6):
        lanes = slice(pair * 128, (pair + 1) * 128)
        keys = k_all[:, lanes]
        head_lane = iota((384, 128), 1)
        keys0 = jnp.where(head_lane < 64, keys, jnp.zeros_like(keys))
        keys1 = jnp.where(head_lane < 64, jnp.zeros_like(keys), keys)
        values = mm_nt(eye, v_all[:, lanes]).astype(BF16)
        scores = [[], []]
        for level in range(12):
            low, high = starts[level], starts[level + 1]
            if level == 0:
                q = q_all[0:128, lanes] * jnp.asarray(0.125, BF16)
            else:
                q = q_exp[pl.ds((level - 1) * 128, 128), lanes]
            both = mm_nt(jnp.concatenate([keys0[low:high], keys1[low:high]], axis=0), q)
            for side in range(2):
                part = both[side * (high - low) : (side + 1) * (high - low)]
                if level:
                    part = part + level * LOG_TWO * (1.0 - slope_ref[2 * pair + side])
                if level < 3:
                    part = jnp.where((seen0, seen1, seen2)[level], part, -jnp.inf)
                scores[side].append(part)
        for side in range(2):
            flat = jnp.concatenate(scores[side], axis=0)
            top = jnp.max(flat, axis=0, keepdims=True)
            powers = jnp.exp(flat - top)
            total = jnp.sum(powers, axis=0, keepdims=True)
            powers = jnp.concatenate([powers, jnp.zeros((16, 128), F32)], axis=0).astype(BF16)
            part = mm(values[side * 64 : (side + 1) * 64], powers)
            attended[pl.ds(pair * 128 + side * 64, 64), :] = (part / total).astype(BF16)
    ready = mm_nt(eye, attended[...]).astype(BF16)
    for pair in range(3):
        o_ref[:, pair * 256 : (pair + 1) * 256] = mm(ready, weights(3, pair)).astype(BF16)

    for made in sent:
        made.wait_send()


COPIES = 80


def shards(features, qkv_flat, out_flat, level_slope):
    vmem = pl.BlockSpec(memory_space=pltpu.VMEM)
    return pl.pallas_call(
        body,
        out_shape=jax.ShapeDtypeStruct((TOK, D), BF16),
        in_specs=[vmem, vmem, vmem, pl.BlockSpec(memory_space=pltpu.SMEM)],
        out_specs=vmem,
        scratch_shapes=[
            pltpu.VMEM((2, RAW, 128), BF16),
            pltpu.VMEM((RAW, 128), F32),
            pltpu.VMEM((16, RAW, 128), BF16),
            pltpu.VMEM((2, NX, NG, SEL_A * KROWS, 128), BF16),
            pltpu.VMEM((2, NG, NX, (SEL - SEL_A) * KROWS, 128), BF16),
            pltpu.VMEM((2, 16, D), BF16),
            pltpu.VMEM((NZ, 16, D), BF16),
            pltpu.VMEM((NY, 16, D), BF16),
            pltpu.VMEM((NX, 16, D), BF16),
            pltpu.VMEM((288, D), BF16),
            pltpu.VMEM((SEL * KROWS, 16 * RAW), BF16),
            pltpu.VMEM((11 * 128, 144), BF16),
            pltpu.VMEM((144, D), BF16),
            pltpu.VMEM((384, D), BF16),
            pltpu.VMEM((384, D), BF16),
            pltpu.VMEM((11 * 128, D), BF16),
            pltpu.VMEM((D, 128), BF16),
            pltpu.SemaphoreType.DMA((COPIES,)),
            pltpu.SemaphoreType.DMA((COPIES,)),
        ],
        compiler_params=pltpu.CompilerParams(
            collective_id=0, has_side_effects=True, vmem_limit_bytes=48 * 2**20
        ),
        name="layer",
    )(features, qkv_flat, out_flat, level_slope)


def solution(mesh):
    in_specs = (P("tm", None), P("tm", None), P("tm", None), P())
    return jax.shard_map(
        shards, mesh=mesh, in_specs=in_specs, out_specs=P("tm", None), check_vma=False
    )
```

time: 446 us -> 72.9 us (0.16); the launches traced: 438 us -> 72.7 us
  waiting for transfers between devices: 242 us -> 0 us
  starting transfers between devices: 84.2 us -> 0 us
  Pallas kernels: 0 us -> 69 us
  local copies, waits for them, and re-layouts: 44.2 us -> 3.64 us
  other arithmetic: 32.8 us -> 0 us
  matrix products: 18.8 us -> 0 us
  between operations: 15.7 us -> 0.01 us
    all_gather x2 -> x0, waiting for transfers between devices: 239 us -> none  [the longest x1 123 us: shards(): lax.all_gather(out_flat, 'tm', axis=0, tiled=True)]
    ppermute x26 -> x0, starting transfers between devices: 84.2 us -> none  [from_partner(): return lax.ppermute(block, axis, route)]
    pallas_call x0 -> x1, Pallas kernels: none -> 69 us  [shards(): pl.pallas_call(body, out_shape=jax.ShapeDtypeStruct((TOK, D), BF16), in_s...]
    reshape x46 -> x0, local copies, waits for them, and re-layouts: 24.8 us -> none  [the longest x1 7.73 us: shards(): qkv_all.reshape(D, 3 * D)]
    dot_general x24 -> x0, matrix products: 18.2 us -> none  [the longest x9 6.18 us: cross_stats(): jnp.einsum('ihd,jhd->ihj', q_heads, k_heads, precision=lax.Precision.HIGH...]
    mul x32 -> x0, other arithmetic: 6.93 us -> none  [the longest x31 5.66 us: pair_mean(): return (halves[:, 0] + halves[:, 1]) * 0.5]
    select_n x24 -> x0, other arithmetic: 5.52 us -> none  [shards(): jnp.where(is_lower, jnp.concatenate([own_part, peer_part]), jnp.concatena...]
    convert_element_type x1 -> x0, other arithmetic: 5.36 us -> none  [shards(): (numerator / denominator[..., None]).reshape(tok_rows, D)]
  transfers between devices with their start and end apart: 28 -> 0, of which waited for: 3 -> 0; matrix products, arithmetic and copies ran while one was open for 13% -> 0% of each run, Pallas kernels for 0% -> 0%
where the time goes in v1:
time: 72.9 us; the launch traced here: 72.7 us
  Pallas kernels  69 us (95%)
  local copies, waits for them, and re-layouts  3.64 us (5%)
    pallas_call x1, Pallas kernels, shards(): pl.pallas_call(body, out_shape=jax.ShapeDtypeStruct((TOK, D), BF16), in_s...  69 us
    unnamed x9, local copies, waits for them, and re-layouts  3.64 us

profile of v1, /device:TPU:1, one launch (start us, length us, event | category | flops | bytes accessed | tf_op | source)
XLA Modules:
  0.0 72.7 jit_solution(17468712308459768509)
XLA Ops:
  0.0 0.0 copy-start
  0.0 0.9 %copy-done = bf16[128,768]{1,0:T(8,128)(2,1)S(1)} copy-done((bf16[128,768]{1,0:T(8,128)(2,1)S(1)}, bf16[128,768]{1,0:T(8,128)(2,1)}, u32[]{:S(2)}) %copy-start) | copy-done | bytes 196632
  0.9 0.0 copy-start.1
  0.9 0.7 copy-done.1
  1.6 0.0 copy-start.2
  1.6 0.7 copy-done.2
  2.3 0.0 copy-start.3
  2.3 0.7 copy-done.3
  3.0 69.0 %layer.1 = bf16[128,768]{1,0:T(8,128)(2,1)S(1)} custom-call(bf16[128,768]{1,0:T(8,128)(2,1)S(1)} %copy-done, bf16[27,128]{1,0:T(8,128)(2,1)S(1)} %copy-done.1, bf16[9,128]{1,0:T(8,128)(2,1)S(1)} %copy-done.2, f32[12]{0:T(128)S(1)} %copy-done.3), custom_call_target="tpu_custom_call" | custom-call | tf_op jit(solution)/shard_map/layer/pallas_call | solution.py:282
  72.0 0.7 copy.6
Async XLA Ops:
  0.0 0.9 %copy-start = (bf16[128,768]{1,0:T(8,128)(2,1)S(1)}, bf16[128,768]{1,0:T(8,128)(2,1)}, u32[]{:S(2)}) copy-start(bf16[128,768]{1,0:T(8,128)(2,1)} %x_ref.1) | copy-start | bytes 589828
  0.9 0.7 copy-start.1
  1.6 0.7 copy-start.2
  2.3 0.7 copy-start.3

commit v2 on v1

v2 whole, which is shorter than its diff:
```python
import math

import jax
import jax.numpy as jnp
from jax import lax
from jax.experimental import pallas as pl
from jax.experimental.pallas import tpu as pltpu
from jax.sharding import PartitionSpec as P

D = 768
HEADS = 12
HEAD_DIM = 64
BLOCK = 16
TOK = 128
NX, NY, NZ = 4, 8, 8
NG = 4
ROWS_Q, ROWS_O = 27, 9
SLOTS = 15
CUT_Q, CUT_O = 128, 80
HALF = D // 2
VMEM_BYTES = 60 * 2**20
LOG_TWO = math.log(2.0)
F32, BF16, I32 = jnp.float32, jnp.bfloat16, jnp.int32
MESH = pl.DeviceIdType.MESH


def iota(shape, dim):
    return lax.broadcasted_iota(I32, shape, dim)


def pick(condition, value=1.0):
    return jnp.where(condition, value, 0.0).astype(BF16)


def mm(a, b):
    return jnp.dot(a, b, preferred_element_type=F32)


def mm_nt(a, b):
    return lax.dot_general(a, b, (((1,), (1,)), ((), ())), preferred_element_type=F32)


def third(value):
    return lax.shift_right_logical(value * 171, 9)


def line_rows(place):
    row, col = iota((64, 128), 0), iota((64, 128), 1)
    r = row & 15
    first = pick((row < 16) & (col == 16 * (place ^ 1) + r))
    second = pick((row >= 16) & (row < 32) & ((col >> 1) == 16 * ((place >> 1) ^ 1) + r), 0.5)
    fourth = pick((row >= 32) & (row < 48) & ((col >> 2) == 16 * ((place >> 2) ^ 1) + r), 0.25)
    whole = pick((row >= 48) & ((col >> 3) == r), 0.125)
    return first + second + fourth + whole


def body(
    x_hbm, qkv_hbm, out_hbm, slope_hbm, o_ref,
    tokens_ref, qkv_ref, out_ref, slope_ref, stage, message, gather_q, gather_o, w_q, w_o,
    feat3, feat4, feat7, feat10,
    rows, order, perm, expand, q_all, k_all, v_all, q_exp, attended, away,
    send, recv, local,
):
    me = lax.axis_index("tm")
    x, y, z, c = me // 128, (me // 16) % 8, (me // 2) % 8, me % 2
    yq, yr, zq, zr = y // 4, y % 4, z // 4, z % 4

    loads = [
        pltpu.make_async_copy(x_hbm, tokens_ref, local.at[0]),
        pltpu.make_async_copy(qkv_hbm, qkv_ref, local.at[1]),
        pltpu.make_async_copy(out_hbm, out_ref, local.at[2]),
        pltpu.make_async_copy(slope_hbm, slope_ref, local.at[3]),
    ]
    for load in loads:
        load.start()

    def at(px, py, pz, pc):
        return ((px * NY + py) * NZ + pz) * 2 + pc

    sibling = at(x, y, z, 1 - c)
    steps = [(2, 2), (2, 1), (1, 2), (2, 3), (3, 2), (1, 1), (1, 3), (3, 1), (3, 3)]
    steps += [(0, 2), (2, 0), (0, 1), (1, 0), (0, 3), (3, 0)]
    square = [at(x, yq * 4 + (yr + j) % 4, zq * 4 + (zr + k) % 4, c) for j, k in steps]
    z_line = [at(x, y, (z + j) % 8, c) for j in (4, 3, 5, 2, 6, 1, 7)]
    y_line = [at(x, (y + j) % 8, z, c) for j in (4, 3, 5, 2, 6, 1, 7)]
    z_rest = [at(x, y, (1 - zq) * 4 + (zr + j) % 4, c) for j in range(4)]
    y_rest = [at(x, (1 - yq) * 4 + (yr + j) % 4, z, c) for j in range(4)]
    x_line = [at((x + j) % 4, y, z, c) for j in (2, 1, 3)]
    opposite, right, left = x_line
    z_mate = at(x, y, (z + 4 * (zr // 2) + 6) % 8, c)
    y_mate = at(x, (y + 4 * (yr // 2) + 6) % 8, z, c)

    barrier = pltpu.get_barrier_semaphore()
    greet = square + z_rest + y_rest + x_line + [sibling]
    for other in greet:
        pl.semaphore_signal(barrier, inc=1, device_id=(other,), device_id_type=MESH)

    sent = []

    def copy(ref, device, target=None):
        slot = len(sent)
        made = pltpu.make_async_remote_copy(
            src_ref=ref, dst_ref=ref if target is None else target, send_sem=send.at[slot], recv_sem=recv.at[slot],
            device_id=(device,), device_id_type=MESH,
        )
        made.start()
        sent.append(made)
        return made

    for load in loads:
        load.wait()
    spot = yr * 4 + zr
    heads = z % 2
    partner = at(x, y, z + 1 - 2 * heads, c)
    stage[...] = jnp.zeros((48, 128), F32)
    stage[0:ROWS_Q, :] = qkv_ref[...].astype(F32)
    stage[32 : 32 + ROWS_O, :] = out_ref[...].astype(F32)
    row, col = iota((32, 32), 0), iota((32, 32), 1)
    half, slot = row >> 4, row & 15
    s = third(slot)
    j = slot - 3 * s
    whole = 9 * c + 6 * s + 3 * half + j
    shared = jnp.where(slot < 12, 18 - 15 * c + 3 * half + j, 24 - 24 * c + j)
    source = jnp.where(slot < 9, whole, shared)
    wanted = (slot < 12) | ((slot < SLOTS) & (half == c))
    message[...] = mm(pick(wanted & (col == source)), stage[0:32, :].astype(BF16)).astype(BF16).reshape(2, 16, 128)
    gather_q[spot] = message[heads]
    gather_o[spot] = stage[32:48, :].astype(BF16)

    pl.semaphore_wait(barrier, len(greet))

    first = [
        copy(message.at[(heads + k) % 2], other, gather_q.at[spot])
        for (j, k), other in zip(steps, square)
    ]

    col = iota((1, D), 1)
    part = third(col >> 4)
    rest = col - 48 * part
    natural = (part >> 2) * 192 + ((part >> 1) & 1) * 96 + (part & 1) * 12
    natural = natural + ((rest >> 2) & 3) * 24 + (rest & 3) * 3 + (rest >> 4)
    order[...] = pick(iota((D, D), 0) == natural)
    tokens = mm(tokens_ref[...], order[...]).astype(BF16)
    rows[0:128, :] = tokens
    row, col = iota((16, 128), 0), iota((16, 128), 1)
    feat3[c] = mm(pick((col >> 3) == row, 0.125), tokens).astype(BF16)
    b = copy(feat3.at[c], sibling)
    row, col = iota((16 * SLOTS, 16 * 16), 0), iota((16 * SLOTS, 16 * 16), 1)
    perm[...] = pick(col == (row & 15) * 16 + (row >> 4))
    for level in range(1, 12):
        row, col = iota((128, 144), 0), iota((128, 144), 1)
        if level < 8:
            hit = (col < 128) & ((col >> level) == (row >> level))
            expand[pl.ds((level - 1) * 128, 128), :] = pick(hit, 0.125 / (1 << level))
        else:
            expand[pl.ds((level - 1) * 128, 128), :] = pick(col == 128 + level - 8, 0.125)

    b.wait_recv()
    mine = pl.ds(pl.multiple_of(c * HALF, 128), HALF)
    row, col = iota((16, 32), 0), iota((16, 32), 1)
    feat4[z] = mm(pick((col >> 1) == row, 0.5), feat3[:, :, mine].reshape(32, HALF)).astype(BF16)
    line = [copy(feat4.at[z], other) for other in z_line]
    second = [copy(gather_o.at[spot], other) for other in square]
    rows[432:448, :] = feat3[1 - c]
    pair3 = copy(feat3.at[1 - c], partner, rows.at[pl.ds(448, 16)])

    for made in first:
        made.wait_recv()
    own = 2 * yq + zq
    w_q[c, x, own] = mm(perm[...], gather_q[...].reshape(16 * 16, 128)).astype(BF16)
    over_z, over_y, far = 2 * yq + 1 - zq, 2 - 2 * yq + zq, 3 - own

    def got(made):
        for one in made:
            one.wait_recv()

    def along(ref):
        return [copy(ref.at[c, x, own], z_mate), copy(ref.at[c, x, own], y_mate)]

    def corner(ref, cut, size):
        return [
            copy(ref.at[c, x, over_z, pl.ds(0, cut)], y_mate),
            copy(ref.at[c, x, over_y, pl.ds(cut, size - cut)], z_mate),
        ]

    def along_x(ref, group, others):
        return [copy(ref.at[c, x, group], other) for other in others]

    def hand_on(ref, group, cut, size):
        return [
            copy(ref.at[c, (x + 3) % 4, group, pl.ds(0, cut)], right),
            copy(ref.at[c, (x + 1) % 4, group, pl.ds(cut, size - cut)], left),
        ]

    def across(ref, px, group):
        return copy(ref.at[c, px, group], sibling)

    yz_q = along(w_q)
    x_q = [along_x(w_q, own, (right, left))]

    got(line)
    z_rows = feat4[...].reshape(128, HALF)
    found = mm(line_rows(z), z_rows).astype(BF16)
    rows[400:416, mine] = found[0:16]
    rows[416:432, mine] = feat4[z]
    rows[288:320, mine] = found[16:48]
    feat7[y] = found[48:]
    line = [copy(feat7.at[y], other) for other in y_line]
    row, col = iota((32, 128), 0), iota((32, 128), 1)
    chip = jnp.where(row < 16, z, z ^ 1)
    row = row & 15
    means = (
        pick((row == 0) & ((col >> 4) == chip), 1 / 16)
        + pick((row == 1) & ((col >> 5) == (z >> 1)), 1 / 32)
        + pick((row == 2) & ((col >> 6) == (z >> 2)), 1 / 64)
        + pick(row == 3, 1 / 128)
    )
    rows[256:288, mine] = mm(means, z_rows).astype(BF16)

    yz_q[0].wait_recv()
    yz_q[1].wait_recv()
    corner_q = corner(w_q, CUT_Q, 16 * SLOTS)
    pair_tokens = copy(rows.at[pl.ds(0, 128)], partner, rows.at[pl.ds(128, 128)])
    x_q.append(along_x(w_q, over_z, (right, left)))
    x_q.append(along_x(w_q, over_y, (right, left)))
    got(x_q[0])
    relay_q = [hand_on(w_q, own, CUT_Q, 16 * SLOTS)]
    over = [across(w_q, (x + 3) % 4, own), across(w_q, (x + 1) % 4, own)]
    got(second)
    w_o[c, x, own] = mm(perm[0 : 16 * ROWS_O, :], gather_o[...].reshape(16 * 16, 128)).astype(BF16)

    got(line)
    found = mm(line_rows(y), feat7[...].reshape(128, HALF)).astype(BF16)
    rows[320:368, mine] = found[:48]
    feat10[x] = found[48:]
    line = [copy(feat10.at[x], other) for other in x_line]

    got(corner_q)
    x_q.append(along_x(w_q, far, (opposite, right, left)))
    over.append(copy(w_q.at[c, x], sibling))
    yz_o = along(w_o)
    for n, group in ((1, over_z), (2, over_y)):
        got(x_q[n])
        relay_q.append(hand_on(w_q, group, CUT_Q, 16 * SLOTS))
        over += [across(w_q, (x + 3) % 4, group), across(w_q, (x + 1) % 4, group)]

    got(line)
    row, col = iota((32, 64), 0), iota((32, 64), 1)
    sides = pick((row < 16) & (col == 16 * (x ^ 1) + row)) + pick(
        (row >= 16) & ((col >> 1) == 16 * ((x >> 1) ^ 1) + row - 16), 0.5
    )
    rows[368:400, mine] = mm(sides, feat10[...].reshape(64, HALF)).astype(BF16)
    coarse = copy(rows.at[pl.ds(256, 176), mine], sibling)

    for made, group in zip(relay_q, (own, over_z, over_y)):
        got(made)
        over.append(across(w_q, (x + 2) % 4, group))
    got(yz_o)
    corner_o = corner(w_o, CUT_O, 16 * ROWS_O)
    x_o = [along_x(w_o, group, x_line) for group in (own, over_z, over_y)]
    x_q[3][1].wait_recv()
    over.append(across(w_q, (x + 3) % 4, far))
    x_q[3][2].wait_recv()
    over.append(across(w_q, (x + 1) % 4, far))
    x_q[3][0].wait_recv()
    over.append(across(w_q, (x + 2) % 4, far))
    coarse.wait_recv()
    pair3.wait_recv()
    pair_tokens.wait_recv()
    got(over)

    def tiles(sources):
        parts = []
        for px in range(NX):
            for group in range(NG):
                for ref, owner, place in sources:
                    parts.append(ref[owner, px, group, place * 16 : place * 16 + 16, :])
        return jnp.concatenate(parts, axis=0)

    def weight_q(s, j):
        second = ((0, 9 + j), (heads, 12 + j), (1, 9 + j))[s]
        return tiles([(w_q, 0, 3 * s + j), (w_q, *second), (w_q, 1, 3 * s + j)])

    def weight_o(n):
        second = (0, 6 + n) if n < 3 else (1, n - 3)
        return tiles([(w_o, 0, n), (w_o, *second), (w_o, 1, 3 + n)])

    row, col = iota((96, 128), 0), iota((96, 128), 1)
    pool = pick((row < 64) & ((col >> 1) == row), 0.5) + pick(
        (row >= 64) & ((col >> 2) == row - 64), 0.25
    )
    made = mm(rows[0:288, :], jnp.concatenate([weight_q(0, j) for j in range(3)], axis=1)).astype(BF16)
    for seg in range(2):
        q_all[seg, 0:128, :] = made[128 * seg : 128 * seg + 128]
        q_all[seg, 128:144, :] = made[256 + 16 * seg : 272 + 16 * seg]
        q_exp[seg] = mm(expand[...], q_all[seg]).astype(BF16)
    for kind, target in ((1, k_all), (2, v_all)):
        made = mm(rows[...], jnp.concatenate([weight_q(kind, j) for j in range(3)], axis=1)).astype(BF16)
        for seg in range(2):
            base = made[128 * seg : 128 * seg + 128]
            target[seg, 0:128, :] = base
            target[seg, 128:224, :] = mm(pool, base).astype(BF16)
            target[seg, 224:336, :] = made[288:400]
            target[seg, 336:352, :] = made[400 + 16 * seg : 416 + 16 * seg]
            target[seg, 352:368, :] = made[432 + 16 * seg : 448 + 16 * seg]
            target[seg, 368:384, :] = jnp.zeros((16, HALF), BF16)

    got(corner_o)
    x_o.append(along_x(w_o, far, x_line))
    over = [copy(w_o.at[c, x], sibling)]

    eye = pick(iota((128, 128), 0) == iota((128, 128), 1))
    lane = iota((128, 128), 1)
    key = iota((128, 128), 0)
    seen0 = (key >> 5) == (lane >> 5)
    seen1 = (key[:64] >> 4) == ((lane[:64] >> 5) ^ 1)
    seen2 = (key[:32] >> 4) == ((lane[:32] >> 6) ^ 1)
    spans = [(0, 0, 128), (1, 128, 192), (2, 192, 224)]
    spans += [(n, 144 + 16 * n, 160 + 16 * n) for n in range(5, 12)] + [(4, 336, 352), (3, 352, 368)]
    back = []
    for seg, pair in [(1, 0), (1, 1), (1, 2), (0, 0), (0, 1), (0, 2)]:
        lanes = slice(pair * 128, (pair + 1) * 128)
        keys = k_all[seg, :, lanes]
        head_lane = iota((384, 128), 1)
        keys0 = jnp.where(head_lane < 64, keys, jnp.zeros_like(keys))
        keys1 = jnp.where(head_lane < 64, jnp.zeros_like(keys), keys)
        values = mm_nt(eye, v_all[seg, :, lanes]).astype(BF16)
        scores = [[], []]
        for level, low, high in spans:
            if level == 0:
                q = q_all[seg, 0:128, lanes] * jnp.asarray(0.125, BF16)
            else:
                q = q_exp[seg, pl.ds((level - 1) * 128, 128), lanes]
            both = mm_nt(jnp.concatenate([keys0[low:high], keys1[low:high]], axis=0), q)
            for side in range(2):
                part = both[side * (high - low) : (side + 1) * (high - low)]
                if level:
                    part = part + level * LOG_TWO * (1.0 - slope_ref[6 * heads + 2 * pair + side])
                if level < 3:
                    part = jnp.where((seen0, seen1, seen2)[level], part, -jnp.inf)
                scores[side].append(part)
        for side in range(2):
            flat = jnp.concatenate(scores[side], axis=0)
            top = jnp.max(flat, axis=0, keepdims=True)
            powers = jnp.exp(flat - top)
            total = jnp.sum(powers, axis=0, keepdims=True)
            powers = jnp.concatenate([powers, jnp.zeros((16, 128), F32)], axis=0).astype(BF16)
            part = mm(values[side * 64 : (side + 1) * 64], powers)
            part = (part / total).astype(BF16)
            if seg:
                away[pl.ds(pair * 128 + side * 64, 64), :] = part
            else:
                attended[heads, pl.ds(pair * 128 + side * 64, 64), :] = part
        if seg:
            piece = pl.ds(pair * 128, 128)
            back.append(copy(away.at[piece], partner, attended.at[heads, piece]))
    got(back)
    ready = mm(mm_nt(eye, attended[...].reshape(D, 128)).astype(BF16), order[...]).astype(BF16)

    for made in x_o:
        got(made)
    over += [copy(w_o.at[c, (x + j) % 4], sibling) for j in (1, 2, 3)]
    got(over)
    for pair in range(3):
        w = jnp.concatenate([weight_o(2 * pair), weight_o(2 * pair + 1)], axis=1)
        o_ref[:, pair * 256 : (pair + 1) * 256] = mm(ready, w).astype(BF16)

    for made in sent:
        made.wait_send()


COPIES = 128


def shards(features, qkv_flat, out_flat, level_slope):
    hbm = pl.BlockSpec(memory_space=pl.ANY)
    return pl.pallas_call(
        body,
        out_shape=jax.ShapeDtypeStruct((TOK, D), BF16),
        in_specs=[hbm] * 4,
        out_specs=pl.BlockSpec(memory_space=pltpu.VMEM),
        scratch_shapes=[
            pltpu.VMEM((TOK, D), BF16),
            pltpu.VMEM((ROWS_Q, 128), BF16),
            pltpu.VMEM((ROWS_O, 128), BF16),
            pltpu.SMEM((HEADS,), F32),
            pltpu.VMEM((48, 128), F32),
            pltpu.VMEM((2, 16, 128), BF16),
            pltpu.VMEM((16, 16, 128), BF16),
            pltpu.VMEM((16, 16, 128), BF16),
            pltpu.VMEM((2, NX, NG, 16 * SLOTS, 128), BF16),
            pltpu.VMEM((2, NX, NG, 16 * ROWS_O, 128), BF16),
            pltpu.VMEM((2, 16, D), BF16),
            pltpu.VMEM((NZ, 16, HALF), BF16),
            pltpu.VMEM((NY, 16, HALF), BF16),
            pltpu.VMEM((NX, 16, HALF), BF16),
            pltpu.VMEM((464, D), BF16),
            pltpu.VMEM((D, D), BF16),
            pltpu.VMEM((16 * SLOTS, 16 * 16), BF16),
            pltpu.VMEM((11 * 128, 144), BF16),
            pltpu.VMEM((2, 144, HALF), BF16),
            pltpu.VMEM((2, 384, HALF), BF16),
            pltpu.VMEM((2, 384, HALF), BF16),
            pltpu.VMEM((2, 11 * 128, HALF), BF16),
            pltpu.VMEM((2, HALF, 128), BF16),
            pltpu.VMEM((HALF, 128), BF16),
            pltpu.SemaphoreType.DMA((COPIES,)),
            pltpu.SemaphoreType.DMA((COPIES,)),
            pltpu.SemaphoreType.DMA((4,)),
        ],
        compiler_params=pltpu.CompilerParams(
            collective_id=0, has_side_effects=True, vmem_limit_bytes=VMEM_BYTES
        ),
        name="layer",
    )(features, qkv_flat, out_flat, level_slope)


def solution(mesh):
    in_specs = (P("tm", None), P("tm", None), P("tm", None), P())
    return jax.shard_map(
        shards, mesh=mesh, in_specs=in_specs, out_specs=P("tm", None), check_vma=False
    )
```

time: 72.9 us -> 53.2 us (0.73)
  the two profiles are of different devices: /device:TPU:1 before, /device:TPU:9 now
where the time goes in v2:
time: 53.2 us; the launch traced here: 53.1 us
  Pallas kernels  51.5 us (97%)
  local copies, waits for them, and re-layouts  1.62 us (3%)
    pallas_call x1, Pallas kernels, shards(): pl.pallas_call(body, out_shape=jax.ShapeDtypeStruct((TOK, D), BF16), in_s...  51.5 us
    unnamed x1, local copies, waits for them, and re-layouts  1.62 us

profile of v2, /device:TPU:9, one launch (start us, length us, event | category | flops | bytes accessed | tf_op | source)
XLA Modules:
  0.0 53.1 jit_solution(5912088765929589776)
XLA Ops:
  0.0 51.5 %layer.1 = bf16[128,768]{1,0:T(8,128)(2,1)} custom-call(bf16[128,768]{1,0:T(8,128)(2,1)} %x_hbm.1, bf16[27,128]{1,0:T(8,128)(2,1)} %qkv_hbm.1, bf16[9,128]{1,0:T(8,128)(2,1)} %out_hbm.1, f32[12]{0:T(128)} %slope_hbm.1), custom_call_target="tpu_custom_call" | custom-call | tf_op jit(solution)/shard_map/layer/pallas_call | solution.py:377
  51.5 1.6 %copy.6 = bf16[128,768]{1,0:T(8,128)(2,1)} copy(bf16[128,768]{1,0:T(8,128)(2,1)} %layer.1) | data formatting | bytes 393216

commit v3 on v2

--- a/solution.py
+++ b/solution.py
@@ -186,17 +186,11 @@
     def along_x(ref, group, others):
         return [copy(ref.at[c, x, group], other) for other in others]
 
-    def hand_on(ref, group, cut, size):
-        return [
-            copy(ref.at[c, (x + 3) % 4, group, pl.ds(0, cut)], right),
-            copy(ref.at[c, (x + 1) % 4, group, pl.ds(cut, size - cut)], left),
-        ]
-
     def across(ref, px, group):
         return copy(ref.at[c, px, group], sibling)
 
     yz_q = along(w_q)
-    x_q = [along_x(w_q, own, (right, left))]
+    x_q = [along_x(w_q, own, (opposite, right, left))]
 
     got(line)
     z_rows = feat4[...].reshape(128, HALF)
@@ -221,11 +215,10 @@
     yz_q[1].wait_recv()
     corner_q = corner(w_q, CUT_Q, 16 * SLOTS)
     pair_tokens = copy(rows.at[pl.ds(0, 128)], partner, rows.at[pl.ds(128, 128)])
-    x_q.append(along_x(w_q, over_z, (right, left)))
-    x_q.append(along_x(w_q, over_y, (right, left)))
+    x_q.append(along_x(w_q, over_z, (opposite, right, left)))
+    x_q.append(along_x(w_q, over_y, (opposite, right, left)))
     got(x_q[0])
-    relay_q = [hand_on(w_q, own, CUT_Q, 16 * SLOTS)]
-    over = [across(w_q, (x + 3) % 4, own), across(w_q, (x + 1) % 4, own)]
+    over = [across(w_q, (x + j) % 4, own) for j in (1, 2, 3)]
     got(second)
     w_o[c, x, own] = mm(perm[0 : 16 * ROWS_O, :], gather_o[...].reshape(16 * 16, 128)).astype(BF16)
 
@@ -241,8 +234,7 @@
     yz_o = along(w_o)
     for n, group in ((1, over_z), (2, over_y)):
         got(x_q[n])
-        relay_q.append(hand_on(w_q, group, CUT_Q, 16 * SLOTS))
-        over += [across(w_q, (x + 3) % 4, group), across(w_q, (x + 1) % 4, group)]
+        over += [across(w_q, (x + j) % 4, group) for j in (1, 2, 3)]
 
     got(line)
     row, col = iota((32, 64), 0), iota((32, 64), 1)
@@ -252,12 +244,8 @@
     rows[368:400, mine] = mm(sides, feat10[...].reshape(64, HALF)).astype(BF16)
     coarse = copy(rows.at[pl.ds(256, 176), mine], sibling)
 
-    for made, group in zip(relay_q, (own, over_z, over_y)):
-        got(made)
-        over.append(across(w_q, (x + 2) % 4, group))
     got(yz_o)
     corner_o = corner(w_o, CUT_O, 16 * ROWS_O)
-    x_o = [along_x(w_o, group, x_line) for group in (own, over_z, over_y)]
     x_q[3][1].wait_recv()
     over.append(across(w_q, (x + 3) % 4, far))
     x_q[3][2].wait_recv()
@@ -267,7 +255,10 @@
     coarse.wait_recv()
     pair3.wait_recv()
     pair_tokens.wait_recv()
+    got(corner_o)
+    x_o = [copy(w_o.at[c, x], other) for other in x_line]
     got(over)
+    over = [copy(w_o.at[c, x], sibling)]
 
     def tiles(sources):
         parts = []
@@ -305,10 +296,6 @@
             target[seg, 352:368, :] = made[432 + 16 * seg : 448 + 16 * seg]
             target[seg, 368:384, :] = jnp.zeros((16, HALF), BF16)
 
-    got(corner_o)
-    x_o.append(along_x(w_o, far, x_line))
-    over = [copy(w_o.at[c, x], sibling)]
-
     eye = pick(iota((128, 128), 0) == iota((128, 128), 1))
     lane = iota((128, 128), 1)
     key = iota((128, 128), 0)
@@ -319,6 +306,9 @@
     spans += [(n, 144 + 16 * n, 160 + 16 * n) for n in range(5, 12)] + [(4, 336, 352), (3, 352, 368)]
     back = []
     for seg, pair in [(1, 0), (1, 1), (1, 2), (0, 0), (0, 1), (0, 2)]:
+        if (seg, pair) == (0, 1):
+            got(x_o)
+            over += [copy(w_o.at[c, (x + j) % 4], sibling) for j in (1, 2, 3)]
         lanes = slice(pair * 128, (pair + 1) * 128)
         keys = k_all[seg, :, lanes]
         head_lane = iota((384, 128), 1)
@@ -357,9 +347,6 @@
     got(back)
     ready = mm(mm_nt(eye, attended[...].reshape(D, 128)).astype(BF16), order[...]).astype(BF16)
 
-    for made in x_o:
-        got(made)
-    over += [copy(w_o.at[c, (x + j) % 4], sibling) for j in (1, 2, 3)]
     got(over)
     for pair in range(3):
         w = jnp.concatenate([weight_o(2 * pair), weight_o(2 * pair + 1)], axis=1)

time: 53.2 us -> 51.4 us (0.966)
  the two profiles are of different devices: /device:TPU:9 before, /device:TPU:1 now
where the time goes in v3:
time: 51.4 us; the launch traced here: 51.2 us
  Pallas kernels  49.6 us (96%)
  local copies, waits for them, and re-layouts  1.62 us (3%)
    pallas_call x1, Pallas kernels, shards(): pl.pallas_call(body, out_shape=jax.ShapeDtypeStruct((TOK, D), BF16), in_s...  49.6 us
    unnamed x1, local copies, waits for them, and re-layouts  1.62 us

profile of v3, /device:TPU:1, one launch (start us, length us, event | category | flops | bytes accessed | tf_op | source)
XLA Modules:
  0.0 51.2 jit_solution(9464084792673790346)
XLA Ops:
  0.0 49.6 %layer.1 = bf16[128,768]{1,0:T(8,128)(2,1)} custom-call(bf16[128,768]{1,0:T(8,128)(2,1)} %x_hbm.1, bf16[27,128]{1,0:T(8,128)(2,1)} %qkv_hbm.1, bf16[9,128]{1,0:T(8,128)(2,1)} %out_hbm.1, f32[12]{0:T(128)} %slope_hbm.1), custom_call_target="tpu_custom_call" | custom-call | tf_op jit(solution)/shard_map/layer/pallas_call | solution.py:364
  49.6 1.6 %copy.6 = bf16[128,768]{1,0:T(8,128)(2,1)} copy(bf16[128,768]{1,0:T(8,128)(2,1)} %layer.1) | data formatting | bytes 393216

commit v4 on v3

--- a/solution.py
+++ b/solution.py
@@ -107,14 +107,12 @@
         sent.append(made)
         return made
 
-    for load in loads:
-        load.wait()
+    loads[1].wait()
     spot = yr * 4 + zr
     heads = z % 2
     partner = at(x, y, z + 1 - 2 * heads, c)
     stage[...] = jnp.zeros((48, 128), F32)
     stage[0:ROWS_Q, :] = qkv_ref[...].astype(F32)
-    stage[32 : 32 + ROWS_O, :] = out_ref[...].astype(F32)
     row, col = iota((32, 32), 0), iota((32, 32), 1)
     half, slot = row >> 4, row & 15
     s = third(slot)
@@ -125,7 +123,6 @@
     wanted = (slot < 12) | ((slot < SLOTS) & (half == c))
     message[...] = mm(pick(wanted & (col == source)), stage[0:32, :].astype(BF16)).astype(BF16).reshape(2, 16, 128)
     gather_q[spot] = message[heads]
-    gather_o[spot] = stage[32:48, :].astype(BF16)
 
     pl.semaphore_wait(barrier, len(greet))
 
@@ -133,6 +130,11 @@
         copy(message.at[(heads + k) % 2], other, gather_q.at[spot])
         for (j, k), other in zip(steps, square)
     ]
+
+    for load in (loads[0], loads[2], loads[3]):
+        load.wait()
+    stage[32 : 32 + ROWS_O, :] = out_ref[...].astype(F32)
+    gather_o[spot] = stage[32:48, :].astype(BF16)
 
     col = iota((1, D), 1)
     part = third(col >> 4)
@@ -252,11 +254,11 @@
     over.append(across(w_q, (x + 1) % 4, far))
     x_q[3][0].wait_recv()
     over.append(across(w_q, (x + 2) % 4, far))
+    got(corner_o)
+    x_o = [copy(w_o.at[c, x], other) for other in x_line]
     coarse.wait_recv()
     pair3.wait_recv()
     pair_tokens.wait_recv()
-    got(corner_o)
-    x_o = [copy(w_o.at[c, x], other) for other in x_line]
     got(over)
     over = [copy(w_o.at[c, x], sibling)]
 

time: 51.4 us -> 51.3 us (level)
  no operation moved by 1% of the time
where the time goes in v4:
time: 51.3 us; the launch traced here: 51.1 us
  Pallas kernels  49.5 us (96%)
  local copies, waits for them, and re-layouts  1.62 us (3%)
    pallas_call x1, Pallas kernels, shards(): pl.pallas_call(body, out_shape=jax.ShapeDtypeStruct((TOK, D), BF16), in_s...  49.5 us
    unnamed x1, local copies, waits for them, and re-layouts  1.62 us

profile of v4, /device:TPU:1, one launch (start us, length us, event | category | flops | bytes accessed | tf_op | source)
XLA Modules:
  0.0 51.1 jit_solution(8133546076873226919)
XLA Ops:
  0.0 49.5 %layer.1 = bf16[128,768]{1,0:T(8,128)(2,1)} custom-call(bf16[128,768]{1,0:T(8,128)(2,1)} %x_hbm.1, bf16[27,128]{1,0:T(8,128)(2,1)} %qkv_hbm.1, bf16[9,128]{1,0:T(8,128)(2,1)} %out_hbm.1, f32[12]{0:T(128)} %slope_hbm.1), custom_call_target="tpu_custom_call" | custom-call | tf_op jit(solution)/shard_map/layer/pallas_call | solution.py:366
  49.5 1.6 %copy.6 = bf16[128,768]{1,0:T(8,128)(2,1)} copy(bf16[128,768]{1,0:T(8,128)(2,1)} %layer.1) | data formatting | bytes 393216

commit v5 on v4

--- a/solution.py
+++ b/solution.py
@@ -78,8 +78,7 @@
         return ((px * NY + py) * NZ + pz) * 2 + pc
 
     sibling = at(x, y, z, 1 - c)
-    steps = [(2, 2), (2, 1), (1, 2), (2, 3), (3, 2), (1, 1), (1, 3), (3, 1), (3, 3)]
-    steps += [(0, 2), (2, 0), (0, 1), (1, 0), (0, 3), (3, 0)]
+    steps = [(j, k) for j in range(4) for k in range(4) if j or k]
     square = [at(x, yq * 4 + (yr + j) % 4, zq * 4 + (zr + k) % 4, c) for j, k in steps]
     z_line = [at(x, y, (z + j) % 8, c) for j in (4, 3, 5, 2, 6, 1, 7)]
     y_line = [at(x, (y + j) % 8, z, c) for j in (4, 3, 5, 2, 6, 1, 7)]

time: 51.3 us -> 51.4 us (level)
  no operation moved by 1% of the time
where the time goes in v5:
time: 51.4 us; the launch traced here: 51.2 us
  Pallas kernels  49.6 us (96%)
  local copies, waits for them, and re-layouts  1.62 us (3%)
    pallas_call x1, Pallas kernels, shards(): pl.pallas_call(body, out_shape=jax.ShapeDtypeStruct((TOK, D), BF16), in_s...  49.6 us
    unnamed x1, local copies, waits for them, and re-layouts  1.62 us

profile of v5, /device:TPU:1, one launch (start us, length us, event | category | flops | bytes accessed | tf_op | source)
XLA Modules:
  0.0 51.2 jit_solution(17180464500402323985)
XLA Ops:
  0.0 49.6 %layer.1 = bf16[128,768]{1,0:T(8,128)(2,1)} custom-call(bf16[128,768]{1,0:T(8,128)(2,1)} %x_hbm.1, bf16[27,128]{1,0:T(8,128)(2,1)} %qkv_hbm.1, bf16[9,128]{1,0:T(8,128)(2,1)} %out_hbm.1, f32[12]{0:T(128)} %slope_hbm.1), custom_call_target="tpu_custom_call" | custom-call | tf_op jit(solution)/shard_map/layer/pallas_call | solution.py:365
  49.6 1.6 %copy.6 = bf16[128,768]{1,0:T(8,128)(2,1)} copy(bf16[128,768]{1,0:T(8,128)(2,1)} %layer.1) | data formatting | bytes 393216
